TPU v7x, 32 devices: a whole 2x2x4 slice. The times are simulated.
32 devices in a mesh: groups: 2 (over x), row: 16 (over z, y, core).
Axes of the slice: x: 2, y: 2, z: 4, core: 2. Of those that a mesh axis runs over, the one named last changes fastest.
Arguments:
- level0_tokens: bfloat16 [256, 128, 256], P(('groups', 'row')), parts along dimension 0, may hold values from -6 to 6
- level0_mod: float32 [6, 256], P('groups'), parts along dimension 0, may hold values from -3 to 3
- level0_qkv: bfloat16 [256, 768], replicated, may hold values from -2 to 2
- level0_out: bfloat16 [256, 256], replicated, may hold values from -0.375 to 0.375
- level0_merge: bfloat16 [1024, 512], replicated, may hold values from -0.1875 to 0.1875
- level1_mod: float32 [6, 512], P('groups'), parts along dimension 0, may hold values from -3 to 3
- level1_qkv: bfloat16 [512, 1536], replicated, may hold values from -2 to 2
- level1_out: bfloat16 [512, 512], replicated, may hold values from -0.25 to 0.25
- level1_merge: bfloat16 [2048, 1024], replicated, may hold values from -0.125 to 0.125
- level2_mod: float32 [6, 1024], P('groups'), parts along dimension 0, may hold values from -3 to 3
- level2_qkv: bfloat16 [1024, 1536], replicated, may hold values from -2 to 2
- level2_out: bfloat16 [512, 1024], replicated, may hold values from -0.25 to 0.25
Outputs:
- level2_result: bfloat16 [64, 32, 1024], P(('groups', 'row')), parts along dimension 0
There are 2 independent parts, one for each index of `groups`. A program takes and returns all parts, laid end to end along the dimension named above; an argument that names none is the same for every part. Nothing has to cross between parts.
All inputs are finite; a program needn't handle non-finite values.
Results may differ from a plain program's by a relative error of at most 0.015.
Values may be sent and summed in bfloat16 or wider, within the bound.
A program may use at most 192 MiB of HBM per device.

v0:
```python
import jax
import jax.numpy as jnp
from jax import lax
from jax.sharding import PartitionSpec as P

DH = 64
HEADS2 = 8


EPSILON = 1e-06
NEGATIVE = -1e30


def padded(cells, sides, width):
    for axis, dim in sides:
        count = lax.axis_size(axis)
        ends = count - 1
        head = lax.slice_in_dim(cells, 0, width, axis=dim)
        tail = lax.slice_in_dim(cells, cells.shape[dim] - width, cells.shape[dim], axis=dim)
        cells = jnp.concatenate(
            [
                lax.ppermute(tail, axis, [(i, (i + 1) % count) for i in range(ends)]),
                cells,
                lax.ppermute(head, axis, [((i + 1) % count, i) for i in range(ends)]),
            ],
            axis=dim,
        )
    return cells


def modulate(tokens, modulation):
    values = tokens.astype(jnp.float32)
    center = values - jnp.mean(values, axis=-1, keepdims=True)
    spread = jnp.mean(center * center, axis=-1, keepdims=True)
    normed = center * lax.rsqrt(spread + EPSILON)
    return (normed * (1.0 + modulation[1]) + modulation[0]).astype(jnp.bfloat16)


def project(tokens, weight):
    return jnp.dot(tokens, weight, preferred_element_type=jnp.float32).astype(jnp.bfloat16)


def residual_gate(tokens, modulation, attended, w_out):
    branch = jnp.dot(attended, w_out, preferred_element_type=jnp.float32)
    return (tokens.astype(jnp.float32) + modulation[2] * branch).astype(jnp.bfloat16)


def merge_tokens(tokens, w_merge):
    row_count, col_count, feat_width = tokens.shape
    folded = tokens.reshape(row_count // 2, 2, col_count // 2, 2, feat_width).transpose(
        0, 2, 1, 3, 4
    )
    folded = folded.reshape(row_count // 2, col_count // 2, 4 * feat_width)
    return project(folded, w_merge)


def window_tiles(queries, kv_ext, head_count, row_start, total_rows):
    row_count, col_count, feat_width = queries.shape
    head_size = feat_width // head_count
    ext_rows = kv_ext.shape[0]
    q_heads = queries.reshape(row_count, col_count, head_count, head_size).transpose(2, 0, 1, 3)
    kv_heads = kv_ext.reshape(ext_rows, col_count, 2, head_count, head_size).transpose(
        2, 3, 0, 1, 4
    )
    col_pad = 0
    block_rows = 1
    while block_rows * col_count < 512 and row_count % (block_rows * 2) == 0:
        block_rows = block_rows * 2
    span_rows = block_rows + 6
    span_cols = col_count + 2 * col_pad
    col_blocks = col_count // col_count
    row_blocks = row_count // block_rows
    q_pos = jnp.arange(block_rows * col_count)
    k_pos = jnp.arange(span_rows * span_cols)
    q_row = q_pos // col_count
    q_col = q_pos % col_count
    k_row = k_pos // span_cols
    k_col = k_pos % span_cols
    row_gap = k_row[None, :] - q_row[:, None]
    col_gap = k_col[None, :] - col_pad - q_col[:, None]
    in_window = (row_gap >= 0) & (row_gap <= 6) & (jnp.abs(col_gap) <= 3)
    q_scale = head_size ** (-0.5)

    def one_block(block_idx):
        first_row = block_idx // col_blocks * block_rows
        first_col = block_idx % col_blocks * col_count
        zero = jnp.zeros((), jnp.int32)
        q_block = lax.dynamic_slice(
            q_heads,
            (zero, first_row, first_col, zero),
            (head_count, block_rows, col_count, head_size),
        )
        q_block = q_block.reshape(head_count, block_rows * col_count, head_size)
        kv_block = lax.dynamic_slice(
            kv_heads,
            (zero, zero, first_row, first_col, zero),
            (2, head_count, span_rows, span_cols, head_size),
        )
        kv_block = kv_block.reshape(2, head_count, span_rows * span_cols, head_size)
        grid_row = row_start + first_row + k_row - 3
        grid_col = first_col + k_col - col_pad
        inside = (
            (grid_row >= 0) & (grid_row < total_rows) & (grid_col >= 0) & (grid_col < col_count)
        )
        allowed = in_window & inside[None, :]
        scores = (
            jnp.einsum("hqd,hkd->hqk", q_block, kv_block[0], preferred_element_type=jnp.float32)
            * q_scale
        )
        scores = jnp.where(allowed[None], scores, NEGATIVE)
        row_max = jnp.max(scores, axis=-1, keepdims=True)
        exponent = jnp.exp(scores - row_max)
        denominator = jnp.sum(exponent, axis=-1)
        attended = jnp.einsum(
            "hqk,hkd->hqd",
            exponent.astype(jnp.bfloat16),
            kv_block[1],
            preferred_element_type=jnp.float32,
        )
        attended = attended / denominator[..., None]
        return attended.astype(jnp.bfloat16).reshape(head_count, block_rows, col_count, head_size)

    block_total = row_blocks * col_blocks
    results = lax.map(one_block, jnp.arange(block_total, dtype=jnp.int32))
    results = results.reshape(row_blocks, col_blocks, head_count, block_rows, col_count, head_size)
    return results.transpose(0, 3, 1, 4, 2, 5).reshape(row_count, col_count, feat_width)


def local_level(tokens, modulation, w_qkv, w_out, level):
    row_count, col_count, feat_width = tokens.shape
    hidden = project(modulate(tokens, modulation), w_qkv)
    queries = hidden[..., :feat_width]
    key_vals = hidden[..., feat_width:]
    if level == 0:
        kv_ext = padded(key_vals, (("row", 0),), 3)
    else:
        kv_ext = padded(key_vals, (("row", 0),), 3)
    row_start = lax.axis_index("row") * row_count
    attended = window_tiles(
        queries, kv_ext, feat_width // DH, row_start, row_count * lax.axis_size("row")
    )
    return residual_gate(tokens, modulation, attended, w_out)


def global_level(tokens, modulation, w_qkv, w_out):
    row_count, col_count, feat_width = tokens.shape
    inner = w_qkv.shape[1] // 3
    local_count = row_count * col_count
    hidden = project(modulate(tokens, modulation), w_qkv).reshape(local_count, 3 * inner)
    q_scale = DH ** (-0.5)
    by_head = hidden.reshape(local_count, 3, HEADS2, DH).transpose(1, 2, 0, 3)
    queries = by_head[0]
    kv_send = by_head[1:].reshape(2 * HEADS2, local_count, DH)
    piece = lax.all_gather(kv_send, "row", axis=1, tiled=True)
    row_max = jnp.full((HEADS2, local_count), NEGATIVE, jnp.float32)
    keys = piece[:HEADS2]
    values = piece[HEADS2:]
    scores = jnp.einsum("hqd,hkd->hqk", queries, keys, preferred_element_type=jnp.float32) * q_scale
    new_max = jnp.maximum(row_max, jnp.max(scores, axis=-1))
    exponent = jnp.exp(scores - new_max[..., None])
    denominator = jnp.sum(exponent, axis=-1)
    summed = jnp.einsum(
        "hqk,hkd->hqd", exponent.astype(jnp.bfloat16), values, preferred_element_type=jnp.float32
    )
    row_max, denominator, summed = (new_max, denominator, summed)
    attended = (
        (summed / denominator[..., None])
        .astype(jnp.bfloat16)
        .transpose(1, 0, 2)
        .reshape(local_count, inner)
    )
    attended = attended.reshape(row_count, col_count, inner)
    return residual_gate(tokens, modulation, attended, w_out)


def on_device(
    level0_tokens,
    level0_mod,
    level0_qkv,
    level0_out,
    level0_merge,
    level1_mod,
    level1_qkv,
    level1_out,
    level1_merge,
    level2_mod,
    level2_qkv,
    level2_out,
):
    fine_out = local_level(level0_tokens, level0_mod, level0_qkv, level0_out, 0)
    middle = merge_tokens(fine_out, level0_merge)
    middle_out = local_level(middle, level1_mod, level1_qkv, level1_out, 1)
    coarse = merge_tokens(middle_out, level1_merge)
    return global_level(coarse, level2_mod, level2_qkv, level2_out)


def solution(mesh):
    return jax.shard_map(
        on_device,
        mesh=mesh,
        in_specs=(
            P(("groups", "row"), None, None),
            P("groups", None),
            P(),
            P(),
            P(),
            P("groups", None),
            P(),
            P(),
            P(),
            P("groups", None),
            P(),
            P(),
        ),
        out_specs=P(("groups", "row"), None, None),
        check_vma=False,
    )
```

profile of v0, /device:TPU:0, one launch (start us, length us, event | category | flops | bytes accessed | tf_op | source)
XLA Modules:
  0.0 222.8 jit_solution(12528295068593089367)
XLA Ops:
  6.5 1.4 fusion.151
  10.7 1.9 convolution_convert_fusion.1
  16.0 3.8 %collective-permute-start = (bf16[3,128,512]{2,1,0:T(8,128)(2,1)}, bf16[3,128,512]{2,1,0:T(8,128)(2,1)}, u32[]{:S(2)}, u32[]{:S(2)}) collective-permute-start(bf16[3,128,512]{2,1,0:T(8,128)(2,1)} %get-tuple-element.277), channel_id=1, source_target_pairs={{0,1},{1,2},{2,3},{3,4},{4,5},{5,6},{6,7},{7,8},{8,9},{9,10},{10,1... | collective-permute-start | bytes 1179656 | tf_op jit(solution)/shard_map/ppermute | solution.py:22
  21.6 1.9 slice.120
  23.4 2.3 %slice.122 = bf16[8,128,512]{2,1,0:T(8,128)(2,1)} slice(bf16[8,128,768]{2,1,0:T(8,128)(2,1)} %copy-done.4), slice={[0:8], [0:128], [256:768]} | slice | bytes 2097152 | tf_op jit(solution)/shard_map/slice | solution.py:133
  25.7 2.1 copy.60
  27.8 1.4 fusion.149
  29.3 2.7 %pad_maximum_fusion = bf16[14,128,512]{2,1,0:T(8,128)(2,1)} fusion(bf16[3,128,512]{2,1,0:T(8,128)(2,1)S(1)} %collective-permute-done.1, bf16[8,128,512]{2,1,0:T(8,128)(2,1)} %slice.122, bf16[3,128,512]{2,1,0:T(8,128)(2,1)} %collective-permute-done), kind=kLoop, calls=%fused_computation.64 | loop fusion | flops 1835008 | bytes 3670016 | tf_op jit(solution)/shard_map/concatenate | solution.py:20
  32.0 4.4 %copy.61 = bf16[14,128,512]{1,0,2:T(8,128)(2,1)} copy(bf16[14,128,512]{2,1,0:T(8,128)(2,1)} %pad_maximum_fusion) | data formatting | bytes 3670016 | tf_op jit(solution)/shard_map/transpose | solution.py:62
  37.0 55.6 %while.19 = (s32[]{:T(128)}, bf16[2,4,4,128,64]{3,4,1,2,0:T(8,128)(2,1)}, s32[2]{0:T(128)}, s32[]{:T(128)}, bf16[4,8,128,64]{2,1,3,0:T(8,128)(2,1)}, /*index=5*/...) while((s32[]{:T(128)}, ...), condition=%wide.region_5.6_spmd.clone.clone, body=%wide.region_2.5_spmd.clone.clone.sunk | while | flops 706107648 | bytes 48554836 | solution.py:124
  38.9 3.8 %constant_dynamic-slice_fusion.5 = (bf16[1,4,10,128,64]{3,2,4,1,0:T(8,128)(2,1)}, bf16[1,4,10,128,64]{3,2,4,1,0:T(8,128)(2,1)}) fusion(bf16[2,4,14,128,64]{3,2,4,1,0:T(8,128)(2,1)} %get-tuple-element.412, s32[]{:T(128)S(6)} %select_n.252, s32[]{:T(128)S(6)} %add.447), kind=kLoop, calls=%fused_computation.39.clone.1 | loop fusion | bytes 2621448 | tf_op jit(solution)/shard_map/while/body/eval_jaxpr/slice | solution.py:107
  42.6 2.2 %squeeze.46 = bf16[4,1280,64]{1,2,0:T(8,128)(2,1)} reshape(bf16[1,4,10,128,64]{3,2,4,1,0:T(8,128)(2,1)} %get-tuple-element.371) | data formatting | bytes 1310720 | tf_op jit(solution)/shard_map/while/body/eval_jaxpr/squeeze | solution.py:117
  44.9 2.8 %fusion.177 = pred[512,1280]{1,0:T(8,128)(4,1)} fusion(s32[512]{0:T(512)} %get-tuple-element.415, s32[1280]{0:T(1024)S(1)} %get-tuple-element.416, s32[512]{0:T(512)} %get-tuple-element.413, s32[1280]{0:T(1024)S(1)} %get-tuple-element.414, pred[1280]{0:T(1024)(128)(4,1)S(1)} %fusion.176), kind=kLoop, calls=%fused_computation.14.clone.1 | loop fusion | flops 5898240 | bytes 670976 | tf_op jit(solution)/shard_map/while/body/eval_jaxpr/and | solution.py:105
  47.6 1.9 constant_dynamic-slice_fusion.6
  50.6 2.2 %squeeze.47 = bf16[4,1280,64]{1,2,0:T(8,128)(2,1)} reshape(bf16[1,4,10,128,64]{3,2,4,1,0:T(8,128)(2,1)} %get-tuple-element.372) | data formatting | bytes 1310720 | tf_op jit(solution)/shard_map/while/body/eval_jaxpr/squeeze | solution.py:107
  52.8 3.6 %fusion.178 = (f32[4,512]{1,0:T(4,128)S(1)}, f32[4,512,1280]{2,1,0:T(8,128)S(1)}) fusion(pred[512,1280]{1,0:T(8,128)(4,1)} %fusion.177, bf16[4,512,64]{1,2,0:T(8,128)(2,1)S(1)} %reshape.375, bf16[4,1280,64]{1,2,0:T(8,128)(2,1)} %squeeze.47), kind=kOutput, calls=%fused_computation.5.clone.1 | convolution fusion | flops 343406592 | bytes 12066816 | tf_op jit(solution)/shard_map/while/body/eval_jaxpr/hqd,hkd->hqk/dot_general | solution.py:107
  56.4 3.1 %fusion.179 = f32[4,512]{1,0:T(4,128)S(1)} fusion(f32[4,512,1280]{2,1,0:T(8,128)S(1)} %get-tuple-element.373, f32[4,512]{1,0:T(4,128)S(1)} %get-tuple-element.374, pred[512,1280]{1,0:T(8,128)(4,1)S(1)} %copy-done.1), kind=kLoop, calls=%fused_computation.6.clone.1 | loop fusion | flops 10483712 | bytes 11157504 | tf_op jit(solution)/shard_map/while/body/eval_jaxpr/reduce_sum | solution.py:113
  59.5 3.5 %fusion.180 = bf16[4,512,64]{1,2,0:T(8,128)(2,1)} fusion(bf16[4,1280,64]{1,2,0:T(8,128)(2,1)S(1)} %copy-done.2, f32[4,512,1280]{2,1,0:T(8,128)S(1)} %get-tuple-element.373, f32[4,512]{1,0:T(4,128)S(1)} %get-tuple-element.374, pred[512,1280]{1,0:T(8,128)(4,1)S(1)} %copy-done.1, f32[4,512]{1,0:T(4,128)S(1)} %fusion.179), kind=kOutput, calls=%fused_computation.17.clone.1 | convolution fusion | flops 346292224 | bytes 12075008 | tf_op jit(solution)/shard_map/while/body/eval_jaxpr/hqk,hkd->hqd/dot_general | solution.py:114
  66.7 3.8 %constant_dynamic-slice_fusion.5 = (bf16[1,4,10,128,64]{3,2,4,1,0:T(8,128)(2,1)}, bf16[1,4,10,128,64]{3,2,4,1,0:T(8,128)(2,1)}) fusion(bf16[2,4,14,128,64]{3,2,4,1,0:T(8,128)(2,1)} %get-tuple-element.412, s32[]{:T(128)S(6)} %select_n.252, s32[]{:T(128)S(6)} %add.447), kind=kLoop, calls=%fused_computation.39.clone.1 | loop fusion | bytes 2621448 | tf_op jit(solution)/shard_map/while/body/eval_jaxpr/slice | solution.py:107
  70.4 2.2 %squeeze.46 = bf16[4,1280,64]{1,2,0:T(8,128)(2,1)} reshape(bf16[1,4,10,128,64]{3,2,4,1,0:T(8,128)(2,1)} %get-tuple-element.371) | data formatting | bytes 1310720 | tf_op jit(solution)/shard_map/while/body/eval_jaxpr/squeeze | solution.py:117
  72.7 2.8 %fusion.177 = pred[512,1280]{1,0:T(8,128)(4,1)} fusion(s32[512]{0:T(512)} %get-tuple-element.415, s32[1280]{0:T(1024)S(1)} %get-tuple-element.416, s32[512]{0:T(512)} %get-tuple-element.413, s32[1280]{0:T(1024)S(1)} %get-tuple-element.414, pred[1280]{0:T(1024)(128)(4,1)S(1)} %fusion.176), kind=kLoop, calls=%fused_computation.14.clone.1 | loop fusion | flops 5898240 | bytes 670976 | tf_op jit(solution)/shard_map/while/body/eval_jaxpr/and | solution.py:105
  75.4 1.9 constant_dynamic-slice_fusion.6
  78.4 2.2 %squeeze.47 = bf16[4,1280,64]{1,2,0:T(8,128)(2,1)} reshape(bf16[1,4,10,128,64]{3,2,4,1,0:T(8,128)(2,1)} %get-tuple-element.372) | data formatting | bytes 1310720 | tf_op jit(solution)/shard_map/while/body/eval_jaxpr/squeeze | solution.py:107
  80.6 3.6 %fusion.178 = (f32[4,512]{1,0:T(4,128)S(1)}, f32[4,512,1280]{2,1,0:T(8,128)S(1)}) fusion(pred[512,1280]{1,0:T(8,128)(4,1)} %fusion.177, bf16[4,512,64]{1,2,0:T(8,128)(2,1)S(1)} %reshape.375, bf16[4,1280,64]{1,2,0:T(8,128)(2,1)} %squeeze.47), kind=kOutput, calls=%fused_computation.5.clone.1 | convolution fusion | flops 343406592 | bytes 12066816 | tf_op jit(solution)/shard_map/while/body/eval_jaxpr/hqd,hkd->hqk/dot_general | solution.py:107
  84.2 3.1 %fusion.179 = f32[4,512]{1,0:T(4,128)S(1)} fusion(f32[4,512,1280]{2,1,0:T(8,128)S(1)} %get-tuple-element.373, f32[4,512]{1,0:T(4,128)S(1)} %get-tuple-element.374, pred[512,1280]{1,0:T(8,128)(4,1)S(1)} %copy-done.1), kind=kLoop, calls=%fused_computation.6.clone.1 | loop fusion | flops 10483712 | bytes 11157504 | tf_op jit(solution)/shard_map/while/body/eval_jaxpr/reduce_sum | solution.py:113
  87.3 3.5 %fusion.180 = bf16[4,512,64]{1,2,0:T(8,128)(2,1)} fusion(bf16[4,1280,64]{1,2,0:T(8,128)(2,1)S(1)} %copy-done.2, f32[4,512,1280]{2,1,0:T(8,128)S(1)} %get-tuple-element.373, f32[4,512]{1,0:T(4,128)S(1)} %get-tuple-element.374, pred[512,1280]{1,0:T(8,128)(4,1)S(1)} %copy-done.1, f32[4,512]{1,0:T(4,128)S(1)} %fusion.179), kind=kOutput, calls=%fused_computation.17.clone.1 | convolution fusion | flops 346292224 | bytes 12075008 | tf_op jit(solution)/shard_map/while/body/eval_jaxpr/hqk,hkd->hqd/dot_general | solution.py:114
  92.6 2.3 %fusion.59 = bf16[8,128,256]{2,1,0:T(8,128)(2,1)} fusion(bf16[8,128,256]{1,2,0:T(8,128)(2,1)} %bitcast.123, bf16[8,128,256]{2,1,0:T(8,128)(2,1)} %param.14, f32[256]{0:T(256)} %bitcast.131, bf16[256,256]{1,0:T(8,128)(2,1)S(1)} %copy-done.8), kind=kOutput, calls=%fused_computation.74 | convolution fusion | flops 135266304 | bytes 1704960 | tf_op jit(solution)/shard_map/dot_general | solution.py:44
  95.0 2.0 reshape.354
  97.0 2.2 copy.45
  99.2 2.2 reshape.355
  101.4 2.0 fusion.152
  105.4 1.5 collective-permute-start.3
  106.8 5.1 %collective-permute-start.2 = (bf16[3,64,1024]{2,1,0:T(8,128)(2,1)}, bf16[3,64,1024]{2,1,0:T(8,128)(2,1)}, u32[]{:S(2)}, u32[]{:S(2)}) collective-permute-start(bf16[3,64,1024]{2,1,0:T(8,128)(2,1)} %get-tuple-element.279), channel_id=1, source_target_pairs={{0,1},{1,2},{2,3},{3,4},{4,5},{5,6},{6,7},{7,8},{8,9},{9,10},{10,1... | collective-permute-start | bytes 1179656 | tf_op jit(solution)/shard_map/ppermute | solution.py:22
  113.9 2.1 reshape.356
  116.0 2.5 %pad_maximum_fusion.1 = bf16[10,64,1024]{2,1,0:T(8,128)(2,1)} fusion(bf16[3,64,1024]{2,1,0:T(8,128)(2,1)} %collective-permute-done.3, bf16[4,64,1024]{2,1,0:T(8,128)(2,1)} %slice.126, bf16[3,64,1024]{2,1,0:T(8,128)(2,1)} %collective-permute-done.2), kind=kLoop, calls=%fused_computation.73 | loop fusion | flops 1310720 | bytes 2621440 | tf_op jit(solution)/shard_map/concatenate | solution.py:20
  118.5 4.4 %reshape.358 = bf16[10,64,2,8,64]{4,3,2,1,0:T(8,128)(2,1)} reshape(bf16[10,64,1024]{2,1,0:T(8,128)(2,1)} %pad_maximum_fusion.1) | data formatting | bytes 2621440 | tf_op jit(solution)/shard_map/reshape | solution.py:62
  122.9 2.4 %copy.89 = bf16[10,64,2,8,64]{4,1,0,3,2:T(8,128)(2,1)S(1)} copy(bf16[10,64,2,8,64]{4,3,2,1,0:T(8,128)(2,1)} %reshape.358) | data formatting | bytes 2621440 | tf_op jit(solution)/shard_map/reshape | solution.py:62
  127.6 1.4 fusion.42
  129.0 2.4 %fusion.94 = bf16[8,256,64]{1,2,0:T(8,128)(2,1)} fusion(bf16[8,640,64]{2,1,0:T(8,128)(2,1)S(1)} %bitcast.120, f32[8,256,640]{2,1,0:T(8,128)S(1)} %get-tuple-element.293, f32[8,256]{1,0:T(8,128)S(1)} %get-tuple-element.292, pred[256,640]{1,0:T(8,128)(4,1)S(1)} %fusion.98, f32[8,256]{1,0:T(8,128)S(1)} %fusion.42), kind=kOutput, calls=%fused_computation.99 | convolution fusion | flops 173277184 | bytes 6340608 | tf_op jit(solution)/shard_map/while/body/eval_jaxpr/hqk,hkd->hqd/dot_general | solution.py:114
  131.4 2.0 reshape.359
  133.5 2.4 %fusion.63 = bf16[4,64,512]{2,1,0:T(8,128)(2,1)} fusion(f32[4,64,512]{2,1,0:T(8,128)} %copy-done.3, bf16[512,512]{1,0:T(8,128)(2,1)} %param.21, bf16[4,64,512]{1,0,2:T(4,128)(2,1)} %bitcast.116, f32[512]{0:T(512)S(1)} %bitcast.127), kind=kOutput, calls=%fused_computation.79 | convolution fusion | flops 134610944 | bytes 1574912 | tf_op jit(solution)/shard_map/dot_general | solution.py:44
  137.8 1.8 reshape.362
  139.6 3.2 %fusion.153 = (f32[2,32]{1,0:T(2,128)S(1)}, f32[2,32,1024]{2,1,0:T(8,128)S(1)}) fusion(bf16[2,32,2048]{2,1,0:T(8,128)(2,1)} %reshape.362, bf16[2048,1024]{1,0:T(8,128)(2,1)} %param.22), kind=kOutput, calls=%fused_computation.193 | convolution fusion | flops 268632000 | bytes 4718848 | tf_op jit(solution)/shard_map/dot_general | solution.py:40
  144.4 1.9 reshape_reshape.6
  149.1 57.9 %all-gather.2.cloned.1.call-done = bf16[16,1024,64]{2,0,1:T(8,128)(2,1)} async-done(((bf16[16,64,64]{2,0,1:T(8,128)(2,1)}), bf16[16,1024,64]{2,0,1:T(8,128)(2,1)}) %all-gather.2.cloned.1.call-update) | async-done | bytes 2097168 | tf_op jit(solution)/shard_map/all_gather | solution.py:154
  207.0 2.5 %fusion.145 = (bf16[8,1024,64]{2,0,1:T(8,128)(2,1)S(1)}, bf16[8,1024,64]{2,0,1:T(8,128)(2,1)S(1)}) fusion(bf16[16,1024,64]{2,0,1:T(8,128)(2,1)} %all-gather.2.cloned.1.call-done), kind=kLoop, calls=%fused_computation.185 | loop fusion | bytes 4194304 | tf_op jit(solution)/shard_map/slice | solution.py:156
  209.5 1.8 multiply_reduce_fusion
  213.7 2.2 fusion.78
  (94 shorter events, 31.1 us)
Async XLA Ops:
  6.5 136.5 %copy-start = (bf16[1024,1536]{1,0:T(8,128)(2,1)S(1)}, bf16[1024,1536]{1,0:T(8,128)(2,1)}, u32[]{:S(2)}) copy-start(bf16[1024,1536]{1,0:T(8,128)(2,1)} %param.24) | copy-start | bytes 9437188
  6.5 200.5 %all-gather.2.cloned.1.call-start = ((), (), s32[]{:S(2)}) async-start(), calls=%async_computation | async-start | bytes 4456448 | tf_op jit(solution)/shard_map/all_gather | solution.py:154
  8.0 12.4 %copy-start.15 = (f32[3,512]{1,0:T(4,128)S(1)}, f32[3,512]{1,0:T(4,128)}, u32[]{:S(2)}) copy-start(f32[3,512]{1,0:T(4,128)} %param.19) | copy-start | bytes 18436
  12.6 1.1 copy-start.4
  14.7 14.6 %collective-permute-start.1 = (bf16[3,128,512]{2,1,0:T(8,128)(2,1)}, bf16[3,128,512]{2,1,0:T(8,128)(2,1)S(1)}, u32[]{:S(2)}, u32[]{:S(2)}) collective-permute-start(bf16[3,128,512]{2,1,0:T(8,128)(2,1)} %get-tuple-element.278), channel_id=1, source_target_pairs={{1,0},{2,1},{3,2},{4,3},{5,4},{6,5},{7,6},{8,7},{9,8},{10,9},{11,1... | collective-permute-start | bytes 1179656 | tf_op jit(solution)/shard_map/ppermute | solution.py:24
  16.0 13.3 %collective-permute-start = (bf16[3,128,512]{2,1,0:T(8,128)(2,1)}, bf16[3,128,512]{2,1,0:T(8,128)(2,1)}, u32[]{:S(2)}, u32[]{:S(2)}) collective-permute-start(bf16[3,128,512]{2,1,0:T(8,128)(2,1)} %get-tuple-element.277), channel_id=1, source_target_pairs={{0,1},{1,2},{2,3},{3,4},{4,5},{5,6},{6,7},{7,8},{8,9},{9,10},{10,1... | collective-permute-start | bytes 1179656 | tf_op jit(solution)/shard_map/ppermute | solution.py:22
  37.0 55.6 %copy-start.8 = (bf16[256,256]{1,0:T(8,128)(2,1)S(1)}, bf16[256,256]{1,0:T(8,128)(2,1)}, u32[]{:S(2)}) copy-start(bf16[256,256]{1,0:T(8,128)(2,1)} %param.17) | copy-start | bytes 393220
  52.8 3.6 %copy-start.1 = (pred[512,1280]{1,0:T(8,128)(4,1)S(1)}, pred[512,1280]{1,0:T(8,128)(4,1)}, u32[]{:S(2)}) copy-start(pred[512,1280]{1,0:T(8,128)(4,1)} %fusion.177) | copy-start | bytes 1966084 | tf_op jit(solution)/shard_map/while
  56.4 3.2 %copy-start.2 = (bf16[4,1280,64]{1,2,0:T(8,128)(2,1)S(1)}, bf16[4,1280,64]{1,2,0:T(8,128)(2,1)}, u32[]{:S(2)}) copy-start(bf16[4,1280,64]{1,2,0:T(8,128)(2,1)} %squeeze.46) | copy-start | bytes 1966084 | tf_op jit(solution)/shard_map/while
  80.6 3.6 %copy-start.1 = (pred[512,1280]{1,0:T(8,128)(4,1)S(1)}, pred[512,1280]{1,0:T(8,128)(4,1)}, u32[]{:S(2)}) copy-start(pred[512,1280]{1,0:T(8,128)(4,1)} %fusion.177) | copy-start | bytes 1966084 | tf_op jit(solution)/shard_map/while
  84.2 3.2 %copy-start.2 = (bf16[4,1280,64]{1,2,0:T(8,128)(2,1)S(1)}, bf16[4,1280,64]{1,2,0:T(8,128)(2,1)}, u32[]{:S(2)}) copy-start(bf16[4,1280,64]{1,2,0:T(8,128)(2,1)} %squeeze.46) | copy-start | bytes 1966084 | tf_op jit(solution)/shard_map/while
  97.0 6.7 %copy-start.13 = (f32[1,512]{1,0:T(1,128)S(1)}, f32[1,512]{1,0:T(1,128)}, u32[]{:S(2)}) copy-start(f32[1,512]{1,0:T(1,128)} %get-tuple-element.285) | copy-start | bytes 6148
  97.0 6.7 %copy-start.14 = (f32[1,512]{1,0:T(1,128)S(1)}, f32[1,512]{1,0:T(1,128)}, u32[]{:S(2)}) copy-start(f32[1,512]{1,0:T(1,128)} %get-tuple-element.286) | copy-start | bytes 6148
  101.4 2.3 %copy-start.7 = (bf16[512,1536]{1,0:T(8,128)(2,1)S(1)}, bf16[512,1536]{1,0:T(8,128)(2,1)}, u32[]{:S(2)}) copy-start(bf16[512,1536]{1,0:T(8,128)(2,1)} %param.20) | copy-start | bytes 4718596
  103.4 9.8 %copy-start.3 = (f32[4,64,512]{2,1,0:T(8,128)}, f32[4,64,512]{2,1,0:T(8,128)S(1)}, u32[]{:S(2)}) copy-start(f32[4,64,512]{2,1,0:T(8,128)S(1)} %get-tuple-element.291) | copy-start | bytes 1572868
  103.4 8.5 %copy-start.16 = (s32[256]{0:T(256)S(1)}, s32[256]{0:T(256)}, u32[]{:S(2)}) copy-start(s32[256]{0:T(256)} %get-tuple-element.304) | copy-start | bytes 3076
  103.4 8.5 %copy-start.17 = (s32[256]{0:T(256)S(1)}, s32[256]{0:T(256)}, u32[]{:S(2)}) copy-start(s32[256]{0:T(256)} %get-tuple-element.305) | copy-start | bytes 3076
  105.4 10.6 %collective-permute-start.3 = (bf16[3,64,1024]{2,1,0:T(8,128)(2,1)}, bf16[3,64,1024]{2,1,0:T(8,128)(2,1)}, u32[]{:S(2)}, u32[]{:S(2)}) collective-permute-start(bf16[3,64,1024]{2,1,0:T(8,128)(2,1)} %get-tuple-element.280), channel_id=1, source_target_pairs={{1,0},{2,1},{3,2},{4,3},{5,4},{6,5},{7,6},{8,7},{9,8},{10,9},{11,1... | collective-permute-start | bytes 1179656 | tf_op jit(solution)/shard_map/ppermute | solution.py:24
  106.8 9.2 %collective-permute-start.2 = (bf16[3,64,1024]{2,1,0:T(8,128)(2,1)}, bf16[3,64,1024]{2,1,0:T(8,128)(2,1)}, u32[]{:S(2)}, u32[]{:S(2)}) collective-permute-start(bf16[3,64,1024]{2,1,0:T(8,128)(2,1)} %get-tuple-element.279), channel_id=1, source_target_pairs={{0,1},{1,2},{2,3},{3,4},{4,5},{5,6},{6,7},{7,8},{8,9},{9,10},{10,1... | collective-permute-start | bytes 1179656 | tf_op jit(solution)/shard_map/ppermute | solution.py:22
  125.3 1.0 copy-start.5
  129.0 4.5 %copy-start.12 = (f32[1,512]{1,0:T(1,128)S(1)}, f32[1,512]{1,0:T(1,128)}, u32[]{:S(2)}) copy-start(f32[1,512]{1,0:T(1,128)} %get-tuple-element.284) | copy-start | bytes 6148
  139.6 3.4 %copy-start.9 = (f32[1,1024]{1,0:T(1,128)S(1)}, f32[1,1024]{1,0:T(1,128)}, u32[]{:S(2)}) copy-start(f32[1,1024]{1,0:T(1,128)} %get-tuple-element.282) | copy-start | bytes 12292
  139.6 3.4 %copy-start.10 = (f32[1,1024]{1,0:T(1,128)S(1)}, f32[1,1024]{1,0:T(1,128)}, u32[]{:S(2)}) copy-start(f32[1,1024]{1,0:T(1,128)} %get-tuple-element.283) | copy-start | bytes 12292
  147.5 0.8 copy-start.6
  211.9 1.8 copy-start.11
Sparse Core Ops, SparseCore 0:
  149.3 57.6 all-gather.1
where the time goes:
time: 224 us; the launch traced here: 223 us
  local copies, waits for them, and re-layouts  74.4 us (33%)
  waiting for transfers between devices  57.9 us (26%)
  matrix products  36.6 us (16%)
  other arithmetic  27.1 us (12%)
  between operations  13.7 us (6%)
  starting transfers between devices  11.7 us (5%)
    all_gather x1, waiting for transfers between devices, global_level(): piece = lax.all_gather(kv_send, 'row', axis=1, tiled=True)  57.9 us
    dot_general x3, matrix products, one_block(): jnp.einsum('hqk,hkd->hqd', exponent.astype(jnp.bfloat16), kv_block[1], pr...  9.45 us
    dot_general x5, matrix products, project(): jnp.dot(tokens, weight, preferred_element_type=jnp.float32)  9.13 us
    ppermute x2, starting transfers between devices, padded(): lax.ppermute(tail, axis, [(i, (i + 1) % count) for i in range(ends)])  8.92 us
    slice x3, local copies, waits for them, and re-layouts, one_block(): kv_block[0]  8.31 us
    dot_general x3, matrix products, one_block(): jnp.einsum('hqd,hkd->hqk', q_block, kv_block[0], preferred_element_type=j...  8.29 us
    reduce_sum x3, other arithmetic, one_block(): denominator = jnp.sum(exponent, axis=-1)  7.73 us
    dot_general x3, matrix products, residual_gate(): branch = jnp.dot(attended, w_out, preferred_element_type=jnp.float32)  6.95 us
  transfers between devices with their start and end apart: 5, of which 1 were waited for; matrix products, arithmetic and copies ran while one was open for 6% of the time, Pallas kernels for 0%

commit v1 on v0

v1 whole, which is shorter than its diff:
```python
import functools

import jax
import jax.numpy as jnp
from jax import lax
from jax.experimental import pallas as pl
from jax.experimental.pallas import tpu as pltpu
from jax.sharding import PartitionSpec as P

DH = 64
HEADS2 = 8
HALO = 3
PAD = 8
TILE = 32
SPAN = TILE + 2 * PAD
LANES = 256
EPSILON = 1e-06
NEGATIVE = -1e30
MESH = pl.DeviceIdType.MESH
F32 = jnp.float32
BF16 = jnp.bfloat16


def modulate(values, mod_ref):
    center = values - jnp.mean(values, axis=-1, keepdims=True)
    spread = jnp.mean(center * center, axis=-1, keepdims=True)
    normed = center * lax.rsqrt(spread + EPSILON)
    return (normed * (1.0 + mod_ref[1:2, :]) + mod_ref[0:1, :]).astype(BF16)


def dot(a, b):
    return jnp.dot(a, b, preferred_element_type=F32)


def dot_t(a, b):
    return lax.dot_general(a, b, (((1,), (1,)), ((), ())), preferred_element_type=F32)


def key_position(count):
    n = lax.broadcasted_iota(jnp.int32, (1, count), 1)
    row = jnp.zeros((1, count), jnp.int32)
    for step in range(1, count // SPAN):
        row = row + (n >= step * SPAN).astype(jnp.int32)
    return row, n - row * SPAN


def window_bias(rows):
    k_row, k_col = key_position((rows + 2 * HALO) * SPAN)
    m = lax.broadcasted_iota(jnp.int32, (rows * TILE, 1), 0)
    row_gap = k_row - m // TILE
    col_gap = k_col - PAD - m % TILE
    near = (row_gap >= 0) & (row_gap <= 2 * HALO) & (col_gap >= -HALO) & (col_gap <= HALO)
    return jnp.where(near, 0.0, NEGATIVE).astype(F32)


def project_rows(x, mod_ref, w_ref, row_count, col_count, first):
    h = modulate(x.reshape(row_count * col_count, x.shape[-1]).astype(F32), mod_ref)
    return dot(h, w_ref[:, first:])


def store_kv(kv, k_ref, v_ref, at, row_count, col_count):
    feat = kv.shape[1] // 2
    zero = jnp.zeros((row_count, PAD, 2 * feat), F32)
    kv = kv.reshape(row_count, col_count, 2 * feat)
    kv = jnp.concatenate([zero, kv, zero], axis=1).astype(BF16)
    k_ref[at : at + row_count] = kv[:, :, :feat]
    v_ref[at : at + row_count] = kv[:, :, feat:]


def attend(q_ref, k_ref, v_ref, o_ref, bias, r0, c0, l0, rows, row_start, total_rows, col_count):
    keys = (rows + 2 * HALO) * SPAN
    m = rows * TILE
    heads = LANES // DH
    lane_head = lax.broadcasted_iota(jnp.int32, (1, LANES), 1) // DH
    k_row, k_col = key_position(keys)
    g_row = row_start + r0 + k_row - HALO
    g_col = c0 + k_col - PAD
    inside = (g_row >= 0) & (g_row < total_rows) & (g_col >= 0) & (g_col < col_count)
    bias = bias + jnp.where(inside, 0.0, NEGATIVE).astype(F32)
    q = q_ref[r0 : r0 + rows, pl.ds(c0, TILE), l0 : l0 + LANES].reshape(m, LANES)
    k = k_ref[r0 : r0 + rows + 2 * HALO, pl.ds(c0, SPAN), l0 : l0 + LANES].reshape(keys, LANES)
    v = v_ref[r0 : r0 + rows + 2 * HALO, pl.ds(c0, SPAN), l0 : l0 + LANES].reshape(keys, LANES)
    out = jnp.zeros((m, LANES), F32)
    stacked = jnp.concatenate(
        [q * (lane_head == h).astype(F32).astype(BF16) for h in range(heads)], axis=0
    )
    s = dot_t(stacked, k).reshape(heads, m, keys) + bias[None]
    top = jnp.max(s, axis=-1, keepdims=True)
    e = jnp.exp(s - top)
    total = jnp.sum(e, axis=-1, keepdims=True)
    o = dot(e.astype(BF16).reshape(heads * m, keys), v).reshape(heads, m, LANES) / total
    for h in range(heads):
        out = jnp.where(lane_head == h, o[h], out)
    o_ref[r0 : r0 + rows, pl.ds(c0, TILE), l0 : l0 + LANES] = out.astype(BF16).reshape(
        rows, TILE, LANES
    )


def gated(x, mod_ref, attended, w_ref):
    return (x.astype(F32) + mod_ref[2:3, :] * dot(attended, w_ref[...])).astype(BF16)


def merge(y, w_ref, row_count, col_count):
    half = col_count // 2
    i = lax.broadcasted_iota(jnp.int32, (col_count, col_count), 0)
    j = lax.broadcasted_iota(jnp.int32, (col_count, col_count), 1)
    source = jnp.where(i < half, 2 * i, 2 * (i - half) + 1)
    pick = (source == j).astype(F32).astype(BF16)
    lines = []
    for r in range(0, row_count, 2):
        parts = []
        for u in (r, r + 1):
            both = dot(pick, y[u * col_count : (u + 1) * col_count]).astype(BF16)
            parts += [both[:half], both[half:]]
        lines.append(jnp.concatenate(parts, axis=1))
    return dot(jnp.concatenate(lines, axis=0), w_ref[...]).astype(BF16)


def remote(src, dst, send, recv, peer):
    return pltpu.make_async_remote_copy(
        src_ref=src, dst_ref=dst, send_sem=send, recv_sem=recv,
        device_id={"row": peer}, device_id_type=MESH,
    )


def halo_copies(n, me, src, dst, send, recv, own_rows, act):
    down = remote(
        src.at[pl.ds(own_rows - HALO, HALO)], dst.at[pl.ds(0, HALO)],
        send.at[0], recv.at[0], jnp.minimum(me + 1, n - 1),
    )
    up = remote(
        src.at[pl.ds(0, HALO)], dst.at[pl.ds(HALO, HALO)],
        send.at[1], recv.at[1], jnp.maximum(me - 1, 0),
    )

    @pl.when(me < n - 1)
    def _():
        if act == "start":
            down.start()
        elif act == "send":
            down.wait_send()
        else:
            up.wait_recv()

    @pl.when(me > 0)
    def _():
        if act == "start":
            up.start()
        elif act == "send":
            up.wait_send()
        else:
            down.wait_recv()


def kernel(
    n,
    tok, mod0, w_qkv0, w_out0, w_merge0, mod1, w_qkv1, w_out1, w_merge1, mod2, w_qkv2, w_out2,
    result,
    qkv0, out0, merge0, qkv1, out1, merge1, qkv2, out2, w_sem,
    x0, x0_halo, q0, k0, v0, a0, x1, x1_halo, q1, k1, v1, a1,
    kv_out, q_out, o_out, kv_all, q_all, o_all,
    h0_send, h0_recv, h1_send, h1_recv, kv_send, kv_recv, q_send, q_recv, o_send, o_recv,
):
    rows0, cols0, feat0 = tok.shape
    rows1, cols1, feat1 = rows0 // 2, cols0 // 2, x1.shape[2]
    rows2, cols2 = rows1 // 2, cols1 // 2
    count2 = rows2 * cols2
    me = lax.axis_index("row")
    scale = DH**-0.5

    own = pltpu.make_async_copy(tok, x0, w_sem.at[8])
    own.start()
    loads = [
        pltpu.make_async_copy(src, dst, w_sem.at[i])
        for i, (src, dst) in enumerate(
            [(w_qkv0, qkv0), (w_out0, out0), (w_merge0, merge0), (w_qkv1, qkv1),
             (w_out1, out1), (w_merge1, merge1), (w_qkv2, qkv2), (w_out2, out2)]
        )
    ]
    for load in loads:
        load.start()

    barrier = pltpu.get_barrier_semaphore()

    def greet(p, carry):
        pl.semaphore_signal(
            barrier, inc=1, device_id={"row": lax.rem(me + p, n)}, device_id_type=MESH
        )
        return carry

    lax.fori_loop(1, n, greet, 0)

    @pl.when(me == 0)
    def _():
        x0_halo[0:HALO] = jnp.zeros((HALO, cols0, feat0), BF16)
        x1_halo[0:HALO] = jnp.zeros((HALO, cols1, feat1), BF16)

    @pl.when(me == n - 1)
    def _():
        x0_halo[HALO:] = jnp.zeros((HALO, cols0, feat0), BF16)
        x1_halo[HALO:] = jnp.zeros((HALO, cols1, feat1), BF16)

    own.wait()
    pl.semaphore_wait(barrier, n - 1)
    halo_copies(n, me, x0, x0_halo, h0_send, h0_recv, rows0, "start")

    loads[0].wait()
    chunk = 4
    for r in range(0, rows0, chunk):
        qkv = project_rows(x0[r : r + chunk], mod0, qkv0, chunk, cols0, 0)
        q0[r : r + chunk] = (
            (qkv[:, :feat0].astype(BF16) * scale).astype(BF16).reshape(chunk, cols0, feat0)
        )
        store_kv(qkv[:, feat0:], k0, v0, HALO + r, chunk, cols0)
    halo_copies(n, me, x0, x0_halo, h0_send, h0_recv, rows0, "recv")
    for r, at in ((0, 0), (HALO, HALO + rows0)):
        kv = project_rows(x0_halo[r : r + HALO], mod0, qkv0, HALO, cols0, feat0)
        store_kv(kv, k0, v0, at, HALO, cols0)

    bias = window_bias(4)

    def fine(t, carry):
        c0 = pl.multiple_of(t * TILE, TILE)
        for r0 in range(0, rows0, 4):
            attend(q0, k0, v0, a0, bias, r0, c0, 0, 4, me * rows0, n * rows0, cols0)
        return carry

    lax.fori_loop(0, cols0 // TILE, fine, 0)
    loads[1].wait()
    loads[2].wait()
    y0 = gated(
        x0[...].reshape(rows0 * cols0, feat0), mod0, a0[...].reshape(rows0 * cols0, feat0), out0
    )
    x1[...] = merge(y0, merge0, rows0, cols0).reshape(rows1, cols1, feat1)

    halo_copies(n, me, x1, x1_halo, h1_send, h1_recv, rows1, "start")
    loads[3].wait()
    qkv = project_rows(x1[...], mod1, qkv1, rows1, cols1, 0)
    q1[...] = (qkv[:, :feat1].astype(BF16) * scale).astype(BF16).reshape(rows1, cols1, feat1)
    store_kv(qkv[:, feat1:], k1, v1, HALO, rows1, cols1)
    halo_copies(n, me, x1, x1_halo, h1_send, h1_recv, rows1, "recv")
    for r, at in ((0, 0), (HALO, HALO + rows1)):
        kv = project_rows(x1_halo[r : r + HALO], mod1, qkv1, HALO, cols1, feat1)
        store_kv(kv, k1, v1, at, HALO, cols1)

    def middle(t, carry):
        c0 = pl.multiple_of(t * TILE, TILE)
        for l0 in range(0, feat1, LANES):
            attend(q1, k1, v1, a1, bias, 0, c0, l0, rows1, me * rows1, n * rows1, cols1)
        return carry

    lax.fori_loop(0, cols1 // TILE, middle, 0)
    loads[4].wait()
    loads[5].wait()
    y1 = gated(
        x1[...].reshape(rows1 * cols1, feat1), mod1, a1[...].reshape(rows1 * cols1, feat1), out1
    )
    x2 = merge(y1, merge1, rows1, cols1)

    loads[6].wait()
    h2 = modulate(x2.astype(F32), mod2)
    inner = HEADS2 * DH
    qkv = dot(h2, qkv2[...])
    slot = lax.rem(me, HEADS2)
    base = me - slot
    blank = jnp.zeros((count2, DH), F32)
    for h in range(HEADS2):
        q = qkv[:, h * DH : (h + 1) * DH].astype(BF16).astype(F32) * scale
        k = qkv[:, inner + h * DH : inner + (h + 1) * DH]
        v = qkv[:, 2 * inner + h * DH : 2 * inner + (h + 1) * DH]
        q_out[h] = jnp.concatenate([q, blank], axis=1).astype(BF16)
        kv_out[h] = jnp.concatenate([k, v], axis=1).astype(BF16)

    def kv_copy(p):
        peer = lax.rem(me + p, n)
        return remote(
            kv_out.at[lax.rem(peer, HEADS2)], kv_all.at[me], kv_send.at[p], kv_recv.at[me], peer
        )

    def kv_from(p):
        peer = lax.rem(me + p, n)
        return remote(kv_out.at[0], kv_all.at[peer], kv_send.at[p], kv_recv.at[peer], peer)

    def q_copy(p):
        other = lax.rem(slot + p, HEADS2)
        return remote(
            q_out.at[other], q_all.at[slot], q_send.at[p], q_recv.at[slot], base + other
        )

    def q_from(p):
        other = lax.rem(slot + p, HEADS2)
        return remote(q_out.at[0], q_all.at[other], q_send.at[p], q_recv.at[other], base + other)

    def o_copy(p):
        other = lax.rem(slot + p, HEADS2)
        return remote(
            o_out.at[other], o_all.at[slot], o_send.at[p], o_recv.at[slot], base + other
        )

    def o_from(p):
        other = lax.rem(slot + p, HEADS2)
        return remote(o_out.at[0], o_all.at[other], o_send.at[p], o_recv.at[other], base + other)

    def each(count, make, act):
        def step(p, carry):
            act(make(p))
            return carry

        lax.fori_loop(1, count, step, 0)

    each(n, kv_copy, lambda c: c.start())
    each(HEADS2, q_copy, lambda c: c.start())
    kv_all[me] = kv_out[slot]
    q_all[slot] = q_out[slot]
    each(HEADS2, q_from, lambda c: c.wait_recv())
    each(n, kv_from, lambda c: c.wait_recv())

    piece = min(n, 16)
    queries = q_all[...].reshape(HEADS2 * count2, 2 * DH)
    block = 128

    def keys_step(t, carry):
        kv = kv_all[pl.ds(t * piece, piece)].reshape(piece * count2, 2 * DH)
        after = []
        for b, (top, total, summed) in enumerate(carry):
            s = dot_t(queries[b * block : (b + 1) * block], kv)
            new = jnp.maximum(top, jnp.max(s, axis=-1, keepdims=True))
            fade = jnp.exp(top - new)
            e = jnp.exp(s - new)
            after.append(
                (
                    new,
                    total * fade + jnp.sum(e, axis=-1, keepdims=True),
                    summed * fade + dot(e.astype(BF16), kv),
                )
            )
        return tuple(after)

    start = tuple(
        (
            jnp.full((block, 1), NEGATIVE, F32),
            jnp.zeros((block, 1), F32),
            jnp.zeros((block, 2 * DH), F32),
        )
        for _ in range(HEADS2 * count2 // block)
    )
    if n == piece:
        done = keys_step(0, start)
    else:
        done = lax.fori_loop(0, n // piece, keys_step, start)
    for b, (top, total, summed) in enumerate(done):
        per = block // count2
        o_out[b * per : (b + 1) * per] = (
            (summed / total).astype(BF16).reshape(per, count2, 2 * DH)
        )
    each(HEADS2, o_copy, lambda c: c.start())
    o_all[slot] = o_out[slot]
    loads[7].wait()
    each(HEADS2, o_from, lambda c: c.wait_recv())
    attended = jnp.concatenate([o_all[h].astype(F32)[:, DH:] for h in range(HEADS2)], axis=1)
    result[...] = gated(x2, mod2, attended.astype(BF16), out2).reshape(rows2, cols2, x2.shape[1])

    halo_copies(n, me, x0, x0_halo, h0_send, h0_recv, rows0, "send")
    halo_copies(n, me, x1, x1_halo, h1_send, h1_recv, rows1, "send")
    each(n, kv_copy, lambda c: c.wait_send())
    each(HEADS2, q_copy, lambda c: c.wait_send())
    each(HEADS2, o_copy, lambda c: c.wait_send())


def on_device(n, *args):
    tok, _, w_qkv0, w_out0, w_merge0, _, w_qkv1, w_out1, w_merge1, _, w_qkv2, w_out2 = args
    rows0, cols0, feat0 = tok.shape
    rows1, cols1, feat1 = rows0 // 2, cols0 // 2, w_merge0.shape[1]
    rows2, cols2, feat2 = rows1 // 2, cols1 // 2, w_merge1.shape[1]
    count2 = rows2 * cols2
    weights = [w_qkv0, w_out0, w_merge0, w_qkv1, w_out1, w_merge1, w_qkv2, w_out2]

    def vm(*shape):
        return pltpu.VMEM(shape, BF16)

    any_spec = pl.BlockSpec(memory_space=pl.ANY)
    vmem = pl.BlockSpec(memory_space=pltpu.VMEM)
    return pl.pallas_call(
        functools.partial(kernel, n),
        out_shape=jax.ShapeDtypeStruct((rows2, cols2, feat2), BF16),
        in_specs=[vmem if i in (1, 5, 9) else any_spec for i in range(12)],
        out_specs=vmem,
        scratch_shapes=[vm(*w.shape) for w in weights]
        + [pltpu.SemaphoreType.DMA((9,))]
        + [
            vm(rows0, cols0, feat0),
            vm(2 * HALO, cols0, feat0),
            vm(rows0, cols0, feat0),
            vm(rows0 + 2 * HALO, cols0 + 2 * PAD, feat0),
            vm(rows0 + 2 * HALO, cols0 + 2 * PAD, feat0),
            vm(rows0, cols0, feat0),
            vm(rows1, cols1, feat1),
            vm(2 * HALO, cols1, feat1),
            vm(rows1, cols1, feat1),
            vm(rows1 + 2 * HALO, cols1 + 2 * PAD, feat1),
            vm(rows1 + 2 * HALO, cols1 + 2 * PAD, feat1),
            vm(rows1, cols1, feat1),
            vm(HEADS2, count2, 2 * DH),
            vm(HEADS2, count2, 2 * DH),
            vm(HEADS2, count2, 2 * DH),
            vm(n, count2, 2 * DH),
            vm(HEADS2, count2, 2 * DH),
            vm(HEADS2, count2, 2 * DH),
        ]
        + [pltpu.SemaphoreType.DMA((2,))] * 4
        + [pltpu.SemaphoreType.DMA((n,))] * 2
        + [pltpu.SemaphoreType.DMA((HEADS2,))] * 4,
        compiler_params=pltpu.CompilerParams(
            collective_id=0, has_side_effects=True, vmem_limit_bytes=56 * 1024 * 1024
        ),
    )(*args)


def solution(mesh):
    return jax.shard_map(
        functools.partial(on_device, mesh.shape["row"]),
        mesh=mesh,
        in_specs=(
            P(("groups", "row"), None, None),
            P("groups", None),
            P(),
            P(),
            P(),
            P("groups", None),
            P(),
            P(),
            P(),
            P("groups", None),
            P(),
            P(),
        ),
        out_specs=P(("groups", "row"), None, None),
        check_vma=False,
    )
```

time: 224 us -> 43 us (0.19)
  local copies, waits for them, and re-layouts: 74.4 us -> 1.57 us
  waiting for transfers between devices: 57.9 us -> 0 us
  Pallas kernels: 0 us -> 41.1 us
  matrix products: 36.6 us -> 0 us
  other arithmetic: 27.1 us -> 0 us
  between operations: 13.7 us -> 0.01 us
  starting transfers between devices: 11.7 us -> 0 us
    all_gather x1 -> x0, waiting for transfers between devices: 57.9 us -> none  [global_level(): piece = lax.all_gather(kv_send, 'row', axis=1, tiled=True)]
    pallas_call x0 -> x1, Pallas kernels: none -> 41.1 us  [on_device(): pl.pallas_call(functools.partial(kernel, n), out_shape=jax.ShapeDtypeStru...]
    dot_general x16 -> x0, matrix products: 36.6 us -> none  [the longest x3 9.45 us: one_block(): jnp.einsum('hqk,hkd->hqd', exponent.astype(jnp.bfloat16), kv_block[1], pr...]
    reshape x11 -> x0, local copies, waits for them, and re-layouts: 21 us -> none  [the longest x2 6.85 us: window_tiles(): kv_ext.reshape(ext_rows, col_count, 2, head_count, head_size)]
    slice x11 -> x0, local copies, waits for them, and re-layouts: 18.5 us -> none  [the longest x3 8.31 us: one_block(): kv_block[0]]
    ppermute x4 -> x0, starting transfers between devices: 11.7 us -> none  [the longest x2 8.92 us: padded(): lax.ppermute(tail, axis, [(i, (i + 1) % count) for i in range(ends)])]
    reduce_sum x8 -> x0, other arithmetic: 11.3 us -> none  [the longest x3 7.73 us: one_block(): denominator = jnp.sum(exponent, axis=-1)]
    transpose x4 -> x0, local copies, waits for them, and re-layouts: 9.64 us -> none  [the longest x1 4.44 us: window_tiles(): kv_ext.reshape(ext_rows, col_count, 2, head_count, head_size)]
  transfers between devices with their start and end apart: 5 -> 0, of which waited for: 1 -> 0; matrix products, arithmetic and copies ran while one was open for 6% -> 0% of each run, Pallas kernels for 0% -> 0%
where the time goes in v1:
time: 43 us; the launch traced here: 42.7 us
  Pallas kernels  41.1 us (96%)
  local copies, waits for them, and re-layouts  1.57 us (4%)
    pallas_call x1, Pallas kernels, on_device(): pl.pallas_call(functools.partial(kernel, n), out_shape=jax.ShapeDtypeStru...  41.1 us
    unnamed x1, local copies, waits for them, and re-layouts  1.57 us

profile of v1, /device:TPU:0, one launch (start us, length us, event | category | flops | bytes accessed | tf_op | source)
XLA Modules:
  0.0 42.7 jit_solution(12908586223927447307)
XLA Ops:
  0.0 41.1 %shard_map.118 = bf16[2,32,1024]{2,1,0:T(8,128)(2,1)} custom-call(bf16[8,128,256]{2,1,0:T(8,128)(2,1)} %tok.1, f32[3,256]{1,0:T(4,128)} %mod0.1, bf16[256,768]{1,0:T(8,128)(2,1)} %w_qkv0.1, bf16[256,256]{1,0:T(8,128)(2,1)} %w_out0.1, bf16[1024,512]{1,0:T(8,128)(2,1)} %w_merge0.1, f32[3,512]{1,0:T(4,128)} %mod1.1, bf16[512,1536]{1,0:T(8,128)(2,1)} %w_qkv1.1, ...), custom_call_target="tpu_custom_call" | custom-call | tf_op jit(solution)/shard_map/pallas_call | solution.py:383
  41.1 1.6 %copy.14 = bf16[2,32,1024]{2,1,0:T(8,128)(2,1)} copy(bf16[2,32,1024]{2,1,0:T(8,128)(2,1)} %shard_map.118) | data formatting | bytes 262144

commit v2 on v1

--- a/solution.py
+++ b/solution.py
@@ -63,8 +63,8 @@
     zero = jnp.zeros((row_count, PAD, 2 * feat), F32)
     kv = kv.reshape(row_count, col_count, 2 * feat)
     kv = jnp.concatenate([zero, kv, zero], axis=1).astype(BF16)
-    k_ref[at : at + row_count] = kv[:, :, :feat]
-    v_ref[at : at + row_count] = kv[:, :, feat:]
+    k_ref[pl.ds(at, row_count)] = kv[:, :, :feat]
+    v_ref[pl.ds(at, row_count)] = kv[:, :, feat:]
 
 
 def attend(q_ref, k_ref, v_ref, o_ref, bias, r0, c0, l0, rows, row_start, total_rows, col_count):
@@ -77,9 +77,9 @@
     g_col = c0 + k_col - PAD
     inside = (g_row >= 0) & (g_row < total_rows) & (g_col >= 0) & (g_col < col_count)
     bias = bias + jnp.where(inside, 0.0, NEGATIVE).astype(F32)
-    q = q_ref[r0 : r0 + rows, pl.ds(c0, TILE), l0 : l0 + LANES].reshape(m, LANES)
-    k = k_ref[r0 : r0 + rows + 2 * HALO, pl.ds(c0, SPAN), l0 : l0 + LANES].reshape(keys, LANES)
-    v = v_ref[r0 : r0 + rows + 2 * HALO, pl.ds(c0, SPAN), l0 : l0 + LANES].reshape(keys, LANES)
+    q = q_ref[pl.ds(r0, rows), pl.ds(c0, TILE), l0 : l0 + LANES].reshape(m, LANES)
+    k = k_ref[pl.ds(r0, rows + 2 * HALO), pl.ds(c0, SPAN), l0 : l0 + LANES].reshape(keys, LANES)
+    v = v_ref[pl.ds(r0, rows + 2 * HALO), pl.ds(c0, SPAN), l0 : l0 + LANES].reshape(keys, LANES)
     out = jnp.zeros((m, LANES), F32)
     stacked = jnp.concatenate(
         [q * (lane_head == h).astype(F32).astype(BF16) for h in range(heads)], axis=0
@@ -91,7 +91,7 @@
     o = dot(e.astype(BF16).reshape(heads * m, keys), v).reshape(heads, m, LANES) / total
     for h in range(heads):
         out = jnp.where(lane_head == h, o[h], out)
-    o_ref[r0 : r0 + rows, pl.ds(c0, TILE), l0 : l0 + LANES] = out.astype(BF16).reshape(
+    o_ref[pl.ds(r0, rows), pl.ds(c0, TILE), l0 : l0 + LANES] = out.astype(BF16).reshape(
         rows, TILE, LANES
     )
 
@@ -123,33 +123,16 @@
     )
 
 
-def halo_copies(n, me, src, dst, send, recv, own_rows, act):
-    down = remote(
-        src.at[pl.ds(own_rows - HALO, HALO)], dst.at[pl.ds(0, HALO)],
-        send.at[0], recv.at[0], jnp.minimum(me + 1, n - 1),
-    )
-    up = remote(
-        src.at[pl.ds(0, HALO)], dst.at[pl.ds(HALO, HALO)],
-        send.at[1], recv.at[1], jnp.maximum(me - 1, 0),
-    )
-
-    @pl.when(me < n - 1)
-    def _():
-        if act == "start":
-            down.start()
-        elif act == "send":
-            down.wait_send()
-        else:
-            up.wait_recv()
-
-    @pl.when(me > 0)
-    def _():
-        if act == "start":
-            up.start()
-        elif act == "send":
-            up.wait_send()
-        else:
-            down.wait_recv()
+def halo_copies(n, me, src, dst, send, recv, down, up):
+    below, above = jnp.minimum(me + 1, n - 1), jnp.maximum(me - 1, 0)
+    made = []
+    for i, (peer, (first, count, at)) in enumerate([(below, p) for p in down] + [(above, p) for p in up]):
+        made.append(
+            remote(
+                src.at[pl.ds(first, count)], dst.at[pl.ds(at, count)], send.at[i], recv.at[i], peer
+            )
+        )
+    return made[: len(down)], made[len(down) :]
 
 
 def kernel(
@@ -177,8 +160,7 @@
              (w_out1, out1), (w_merge1, merge1), (w_qkv2, qkv2), (w_out2, out2)]
         )
     ]
-    for load in loads:
-        load.start()
+    loads[0].start()
 
     barrier = pltpu.get_barrier_semaphore()
 
@@ -202,43 +184,97 @@
 
     own.wait()
     pl.semaphore_wait(barrier, n - 1)
-    halo_copies(n, me, x0, x0_halo, h0_send, h0_recv, rows0, "start")
+    has_below, has_above = me < n - 1, me > 0
+    down0, up0 = halo_copies(
+        n, me, x0, x0_halo, h0_send, h0_recv, [(rows0 - HALO, HALO, 0)], [(0, HALO, HALO)]
+    )
+    early, late = rows1 // 2, rows1 - HALO
+    down1, up1 = halo_copies(
+        n, me, x1, x1_halo, h1_send, h1_recv,
+        [(late, early - late, 0), (early, rows1 - early, early - late)],
+        [(0, early, HALO), (early, HALO - early, HALO + early)],
+    )
+
+    @pl.when(has_below)
+    def _():
+        down0[0].start()
+
+    @pl.when(has_above)
+    def _():
+        up0[0].start()
 
     loads[0].wait()
-    chunk = 4
+    for load in loads[1:]:
+        load.start()
+    chunk = rows0 // 2
     for r in range(0, rows0, chunk):
         qkv = project_rows(x0[r : r + chunk], mod0, qkv0, chunk, cols0, 0)
         q0[r : r + chunk] = (
             (qkv[:, :feat0].astype(BF16) * scale).astype(BF16).reshape(chunk, cols0, feat0)
         )
         store_kv(qkv[:, feat0:], k0, v0, HALO + r, chunk, cols0)
-    halo_copies(n, me, x0, x0_halo, h0_send, h0_recv, rows0, "recv")
-    for r, at in ((0, 0), (HALO, HALO + rows0)):
-        kv = project_rows(x0_halo[r : r + HALO], mod0, qkv0, HALO, cols0, feat0)
-        store_kv(kv, k0, v0, at, HALO, cols0)
-
-    bias = window_bias(4)
-
-    def fine(t, carry):
-        c0 = pl.multiple_of(t * TILE, TILE)
-        for r0 in range(0, rows0, 4):
-            attend(q0, k0, v0, a0, bias, r0, c0, 0, 4, me * rows0, n * rows0, cols0)
-        return carry
-
-    lax.fori_loop(0, cols0 // TILE, fine, 0)
-    loads[1].wait()
-    loads[2].wait()
-    y0 = gated(
-        x0[...].reshape(rows0 * cols0, feat0), mod0, a0[...].reshape(rows0 * cols0, feat0), out0
-    )
-    x1[...] = merge(y0, merge0, rows0, cols0).reshape(rows1, cols1, feat1)
-
-    halo_copies(n, me, x1, x1_halo, h1_send, h1_recv, rows1, "start")
+
+    bias = window_bias(chunk)
+    first = 1 - lax.rem(me, 2)
+    for part in range(2):
+        half = first if part == 0 else 1 - first
+        r0 = half * chunk
+
+        @pl.when(has_below & (half == 1))
+        def _():
+            up0[0].wait_recv()
+
+        @pl.when(has_above & (half == 0))
+        def _():
+            down0[0].wait_recv()
+
+        kv = project_rows(x0_halo[pl.ds(half * HALO, HALO)], mod0, qkv0, HALO, cols0, feat0)
+        store_kv(kv, k0, v0, half * (HALO + rows0), HALO, cols0)
+
+        def fine(t, carry):
+            for u in range(2):
+                c0 = pl.multiple_of(t * (2 * TILE) + u * TILE, TILE)
+                attend(
+                    q0, k0, v0, a0, bias, r0, c0, 0, chunk, me * rows0, n * rows0, cols0
+                )
+            return carry
+
+        lax.fori_loop(0, cols0 // (2 * TILE), fine, 0)
+        if part == 0:
+            loads[1].wait()
+            loads[2].wait()
+        y0 = gated(
+            x0[pl.ds(r0, chunk)].reshape(chunk * cols0, feat0), mod0,
+            a0[pl.ds(r0, chunk)].reshape(chunk * cols0, feat0), out0,
+        )
+        x1[pl.ds(half * early, early)] = merge(y0, merge0, chunk, cols0).reshape(
+            early, cols1, feat1
+        )
+        for side in range(2):
+
+            @pl.when(has_below & (half == side))
+            def _():
+                down1[side].start()
+
+            @pl.when(has_above & (half == side))
+            def _():
+                up1[side].start()
+
     loads[3].wait()
     qkv = project_rows(x1[...], mod1, qkv1, rows1, cols1, 0)
     q1[...] = (qkv[:, :feat1].astype(BF16) * scale).astype(BF16).reshape(rows1, cols1, feat1)
     store_kv(qkv[:, feat1:], k1, v1, HALO, rows1, cols1)
-    halo_copies(n, me, x1, x1_halo, h1_send, h1_recv, rows1, "recv")
+
+    @pl.when(has_above)
+    def _():
+        down1[0].wait_recv()
+        down1[1].wait_recv()
+
+    @pl.when(has_below)
+    def _():
+        up1[0].wait_recv()
+        up1[1].wait_recv()
+
     for r, at in ((0, 0), (HALO, HALO + rows1)):
         kv = project_rows(x1_halo[r : r + HALO], mod1, qkv1, HALO, cols1, feat1)
         store_kv(kv, k1, v1, at, HALO, cols1)
@@ -260,15 +296,13 @@
     loads[6].wait()
     h2 = modulate(x2.astype(F32), mod2)
     inner = HEADS2 * DH
-    qkv = dot(h2, qkv2[...])
     slot = lax.rem(me, HEADS2)
     base = me - slot
     blank = jnp.zeros((count2, DH), F32)
+    kv = dot(h2, qkv2[:, inner:])
     for h in range(HEADS2):
-        q = qkv[:, h * DH : (h + 1) * DH].astype(BF16).astype(F32) * scale
-        k = qkv[:, inner + h * DH : inner + (h + 1) * DH]
-        v = qkv[:, 2 * inner + h * DH : 2 * inner + (h + 1) * DH]
-        q_out[h] = jnp.concatenate([q, blank], axis=1).astype(BF16)
+        k = kv[:, h * DH : (h + 1) * DH]
+        v = kv[:, inner + h * DH : inner + (h + 1) * DH]
         kv_out[h] = jnp.concatenate([k, v], axis=1).astype(BF16)
 
     def kv_copy(p):
@@ -291,15 +325,14 @@
         other = lax.rem(slot + p, HEADS2)
         return remote(q_out.at[0], q_all.at[other], q_send.at[p], q_recv.at[other], base + other)
 
-    def o_copy(p):
-        other = lax.rem(slot + p, HEADS2)
+    def o_copy(other):
         return remote(
-            o_out.at[other], o_all.at[slot], o_send.at[p], o_recv.at[slot], base + other
+            o_out.at[other], o_all.at[slot], o_send.at[other], o_recv.at[slot], base + other
         )
 
     def o_from(p):
         other = lax.rem(slot + p, HEADS2)
-        return remote(o_out.at[0], o_all.at[other], o_send.at[p], o_recv.at[other], base + other)
+        return remote(o_out.at[0], o_all.at[other], o_send.at[other], o_recv.at[other], base + other)
 
     def each(count, make, act):
         def step(p, carry):
@@ -309,6 +342,9 @@
         lax.fori_loop(1, count, step, 0)
 
     each(n, kv_copy, lambda c: c.start())
+    q = dot(h2, qkv2[:, :inner]).astype(BF16).astype(F32) * scale
+    for h in range(HEADS2):
+        q_out[h] = jnp.concatenate([q[:, h * DH : (h + 1) * DH], blank], axis=1).astype(BF16)
     each(HEADS2, q_copy, lambda c: c.start())
     kv_all[me] = kv_out[slot]
     q_all[slot] = q_out[slot]
@@ -319,52 +355,60 @@
     queries = q_all[...].reshape(HEADS2 * count2, 2 * DH)
     block = 128
 
-    def keys_step(t, carry):
-        kv = kv_all[pl.ds(t * piece, piece)].reshape(piece * count2, 2 * DH)
-        after = []
-        for b, (top, total, summed) in enumerate(carry):
-            s = dot_t(queries[b * block : (b + 1) * block], kv)
+    for b in range(HEADS2 * count2 // block):
+        asked = queries[b * block : (b + 1) * block]
+
+        def keys_step(t, carry):
+            top, total, summed = carry
+            kv = kv_all[pl.ds(t * piece, piece)].reshape(piece * count2, 2 * DH)
+            s = dot_t(asked, kv)
             new = jnp.maximum(top, jnp.max(s, axis=-1, keepdims=True))
             fade = jnp.exp(top - new)
             e = jnp.exp(s - new)
-            after.append(
-                (
-                    new,
-                    total * fade + jnp.sum(e, axis=-1, keepdims=True),
-                    summed * fade + dot(e.astype(BF16), kv),
-                )
+            return (
+                new,
+                total * fade + jnp.sum(e, axis=-1, keepdims=True),
+                summed * fade + dot(e.astype(BF16), kv),
             )
-        return tuple(after)
-
-    start = tuple(
-        (
+
+        start = (
             jnp.full((block, 1), NEGATIVE, F32),
             jnp.zeros((block, 1), F32),
             jnp.zeros((block, 2 * DH), F32),
         )
-        for _ in range(HEADS2 * count2 // block)
-    )
-    if n == piece:
-        done = keys_step(0, start)
-    else:
-        done = lax.fori_loop(0, n // piece, keys_step, start)
-    for b, (top, total, summed) in enumerate(done):
+        if n == piece:
+            _, total, summed = keys_step(0, start)
+        else:
+            _, total, summed = lax.fori_loop(0, n // piece, keys_step, start)
         per = block // count2
         o_out[b * per : (b + 1) * per] = (
             (summed / total).astype(BF16).reshape(per, count2, 2 * DH)
         )
-    each(HEADS2, o_copy, lambda c: c.start())
+        for other in range(b * per, (b + 1) * per):
+
+            @pl.when(other != slot)
+            def _():
+                o_copy(other).start()
+
     o_all[slot] = o_out[slot]
     loads[7].wait()
     each(HEADS2, o_from, lambda c: c.wait_recv())
     attended = jnp.concatenate([o_all[h].astype(F32)[:, DH:] for h in range(HEADS2)], axis=1)
     result[...] = gated(x2, mod2, attended.astype(BF16), out2).reshape(rows2, cols2, x2.shape[1])
 
-    halo_copies(n, me, x0, x0_halo, h0_send, h0_recv, rows0, "send")
-    halo_copies(n, me, x1, x1_halo, h1_send, h1_recv, rows1, "send")
+    @pl.when(has_below)
+    def _():
+        for copy in (down0[0], down1[0], down1[1]):
+            copy.wait_send()
+
+    @pl.when(has_above)
+    def _():
+        for copy in (up0[0], up1[0], up1[1]):
+            copy.wait_send()
+
     each(n, kv_copy, lambda c: c.wait_send())
     each(HEADS2, q_copy, lambda c: c.wait_send())
-    each(HEADS2, o_copy, lambda c: c.wait_send())
+    each(HEADS2, o_from, lambda c: c.wait_send())
 
 
 def on_device(n, *args):
@@ -407,7 +451,7 @@
             vm(HEADS2, count2, 2 * DH),
             vm(HEADS2, count2, 2 * DH),
         ]
-        + [pltpu.SemaphoreType.DMA((2,))] * 4
+        + [pltpu.SemaphoreType.DMA((4,))] * 4
         + [pltpu.SemaphoreType.DMA((n,))] * 2
         + [pltpu.SemaphoreType.DMA((HEADS2,))] * 4,
         compiler_params=pltpu.CompilerParams(

time: 43 us -> 38.5 us (0.90)
  Pallas kernels: 41.1 us -> 36.6 us
    pallas_call x1, Pallas kernels: 41.1 us -> 36.6 us  [on_device(): pl.pallas_call(functools.partial(kernel, n), out_shape=jax.ShapeDtypeStru...]
where the time goes in v2:
time: 38.5 us; the launch traced here: 38.2 us
  Pallas kernels  36.6 us (95%)
  local copies, waits for them, and re-layouts  1.57 us (4%)
    pallas_call x1, Pallas kernels, on_device(): pl.pallas_call(functools.partial(kernel, n), out_shape=jax.ShapeDtypeStru...  36.6 us
    unnamed x1, local copies, waits for them, and re-layouts  1.57 us

profile of v2, /device:TPU:0, one launch (start us, length us, event | category | flops | bytes accessed | tf_op | source)
XLA Modules:
  0.0 38.2 jit_solution(5796879067959523621)
XLA Ops:
  0.0 36.6 %shard_map.118 = bf16[2,32,1024]{2,1,0:T(8,128)(2,1)} custom-call(bf16[8,128,256]{2,1,0:T(8,128)(2,1)} %tok.1, f32[3,256]{1,0:T(4,128)} %mod0.1, bf16[256,768]{1,0:T(8,128)(2,1)} %w_qkv0.1, bf16[256,256]{1,0:T(8,128)(2,1)} %w_out0.1, bf16[1024,512]{1,0:T(8,128)(2,1)} %w_merge0.1, f32[3,512]{1,0:T(4,128)} %mod1.1, bf16[512,1536]{1,0:T(8,128)(2,1)} %w_qkv1.1, ...), custom_call_target="tpu_custom_call" | custom-call | tf_op jit(solution)/shard_map/pallas_call | solution.py:427
  36.6 1.6 %copy.14 = bf16[2,32,1024]{2,1,0:T(8,128)(2,1)} copy(bf16[2,32,1024]{2,1,0:T(8,128)(2,1)} %shard_map.118) | data formatting | bytes 262144

commit v3 on v2

--- a/solution.py
+++ b/solution.py
@@ -275,9 +275,9 @@
         up1[0].wait_recv()
         up1[1].wait_recv()
 
-    for r, at in ((0, 0), (HALO, HALO + rows1)):
-        kv = project_rows(x1_halo[r : r + HALO], mod1, qkv1, HALO, cols1, feat1)
-        store_kv(kv, k1, v1, at, HALO, cols1)
+    kv = project_rows(x1_halo[...], mod1, qkv1, 2 * HALO, cols1, feat1)
+    store_kv(kv[: HALO * cols1], k1, v1, 0, HALO, cols1)
+    store_kv(kv[HALO * cols1 :], k1, v1, HALO + rows1, HALO, cols1)
 
     def middle(t, carry):
         c0 = pl.multiple_of(t * TILE, TILE)
@@ -298,7 +298,7 @@
     inner = HEADS2 * DH
     slot = lax.rem(me, HEADS2)
     base = me - slot
-    blank = jnp.zeros((count2, DH), F32)
+    pair = count2 // 2
     kv = dot(h2, qkv2[:, inner:])
     for h in range(HEADS2):
         k = kv[:, h * DH : (h + 1) * DH]
@@ -341,10 +341,21 @@
 
         lax.fori_loop(1, count, step, 0)
 
-    each(n, kv_copy, lambda c: c.start())
+
+    def far_first(i, carry):
+        p = lax.rem(i + n // 2 - HEADS2 // 2, n)
+
+        @pl.when(p > 0)
+        def _():
+            kv_copy(p).start()
+
+        return carry
+
+    lax.fori_loop(0, n, far_first, 0)
     q = dot(h2, qkv2[:, :inner]).astype(BF16).astype(F32) * scale
     for h in range(HEADS2):
-        q_out[h] = jnp.concatenate([q[:, h * DH : (h + 1) * DH], blank], axis=1).astype(BF16)
+        mine = q[:, h * DH : (h + 1) * DH]
+        q_out[h] = jnp.concatenate([mine[:pair], mine[pair:]], axis=1).astype(BF16)
     each(HEADS2, q_copy, lambda c: c.start())
     kv_all[me] = kv_out[slot]
     q_all[slot] = q_out[slot]
@@ -352,7 +363,16 @@
     each(n, kv_from, lambda c: c.wait_recv())
 
     piece = min(n, 16)
-    queries = q_all[...].reshape(HEADS2 * count2, 2 * DH)
+    packed = q_all[...].astype(F32)
+    blank = jnp.zeros((HEADS2, pair, DH), F32)
+    queries = jnp.concatenate(
+        [
+            jnp.concatenate([packed[:, :, :DH], blank], axis=2),
+            jnp.concatenate([packed[:, :, DH:], blank], axis=2),
+        ],
+        axis=1,
+    )
+    queries = queries.astype(BF16).reshape(HEADS2 * count2, 2 * DH)
     block = 128
 
     for b in range(HEADS2 * count2 // block):
@@ -381,9 +401,10 @@
         else:
             _, total, summed = lax.fori_loop(0, n // piece, keys_step, start)
         per = block // count2
-        o_out[b * per : (b + 1) * per] = (
-            (summed / total).astype(BF16).reshape(per, count2, 2 * DH)
-        )
+        o = (summed / total).reshape(per, count2, 2 * DH)
+        o_out[b * per : (b + 1) * per] = jnp.concatenate(
+            [o[:, :pair, DH:], o[:, pair:, DH:]], axis=2
+        ).astype(BF16)
         for other in range(b * per, (b + 1) * per):
 
             @pl.when(other != slot)
@@ -393,7 +414,14 @@
     o_all[slot] = o_out[slot]
     loads[7].wait()
     each(HEADS2, o_from, lambda c: c.wait_recv())
-    attended = jnp.concatenate([o_all[h].astype(F32)[:, DH:] for h in range(HEADS2)], axis=1)
+    packed = o_all[...].astype(F32)
+    attended = jnp.concatenate(
+        [
+            jnp.concatenate([packed[h, :, :DH], packed[h, :, DH:]], axis=0)
+            for h in range(HEADS2)
+        ],
+        axis=1,
+    )
     result[...] = gated(x2, mod2, attended.astype(BF16), out2).reshape(rows2, cols2, x2.shape[1])
 
     @pl.when(has_below)
@@ -445,11 +473,11 @@
             vm(rows1 + 2 * HALO, cols1 + 2 * PAD, feat1),
             vm(rows1, cols1, feat1),
             vm(HEADS2, count2, 2 * DH),
-            vm(HEADS2, count2, 2 * DH),
-            vm(HEADS2, count2, 2 * DH),
+            vm(HEADS2, count2 // 2, 2 * DH),
+            vm(HEADS2, count2 // 2, 2 * DH),
             vm(n, count2, 2 * DH),
-            vm(HEADS2, count2, 2 * DH),
-            vm(HEADS2, count2, 2 * DH),
+            vm(HEADS2, count2 // 2, 2 * DH),
+            vm(HEADS2, count2 // 2, 2 * DH),
         ]
         + [pltpu.SemaphoreType.DMA((4,))] * 4
         + [pltpu.SemaphoreType.DMA((n,))] * 2

time: 38.5 us -> 38.1 us (0.990)
  Pallas kernels: 36.6 us -> 36.2 us
    pallas_call x1, Pallas kernels: 36.6 us -> 36.2 us  [on_device(): pl.pallas_call(functools.partial(kernel, n), out_shape=jax.ShapeDtypeStru...]
where the time goes in v3:
time: 38.1 us; the launch traced here: 37.8 us
  Pallas kernels  36.2 us (95%)
  local copies, waits for them, and re-layouts  1.57 us (4%)
    pallas_call x1, Pallas kernels, on_device(): pl.pallas_call(functools.partial(kernel, n), out_shape=jax.ShapeDtypeStru...  36.2 us
    unnamed x1, local copies, waits for them, and re-layouts  1.57 us

profile of v3, /device:TPU:0, one launch (start us, length us, event | category | flops | bytes accessed | tf_op | source)
XLA Modules:
  0.0 37.8 jit_solution(12453690838297214120)
XLA Ops:
  0.0 36.2 %shard_map.118 = bf16[2,32,1024]{2,1,0:T(8,128)(2,1)} custom-call(bf16[8,128,256]{2,1,0:T(8,128)(2,1)} %tok.1, f32[3,256]{1,0:T(4,128)} %mod0.1, bf16[256,768]{1,0:T(8,128)(2,1)} %w_qkv0.1, bf16[256,256]{1,0:T(8,128)(2,1)} %w_out0.1, bf16[1024,512]{1,0:T(8,128)(2,1)} %w_merge0.1, f32[3,512]{1,0:T(4,128)} %mod1.1, bf16[512,1536]{1,0:T(8,128)(2,1)} %w_qkv1.1, ...), custom_call_target="tpu_custom_call" | custom-call | tf_op jit(solution)/shard_map/pallas_call | solution.py:455
  36.2 1.6 %copy.14 = bf16[2,32,1024]{2,1,0:T(8,128)(2,1)} copy(bf16[2,32,1024]{2,1,0:T(8,128)(2,1)} %shard_map.118) | data formatting | bytes 262144

commit v4 on v3

--- a/solution.py
+++ b/solution.py
@@ -88,9 +88,10 @@
     top = jnp.max(s, axis=-1, keepdims=True)
     e = jnp.exp(s - top)
     total = jnp.sum(e, axis=-1, keepdims=True)
-    o = dot(e.astype(BF16).reshape(heads * m, keys), v).reshape(heads, m, LANES) / total
+    share = 1.0 / total
+    o = dot(e.astype(BF16).reshape(heads * m, keys), v).reshape(heads, m, LANES)
     for h in range(heads):
-        out = jnp.where(lane_head == h, o[h], out)
+        out = jnp.where(lane_head == h, o[h] * share[h], out)
     o_ref[pl.ds(r0, rows), pl.ds(c0, TILE), l0 : l0 + LANES] = out.astype(BF16).reshape(
         rows, TILE, LANES
     )
@@ -279,13 +280,9 @@
     store_kv(kv[: HALO * cols1], k1, v1, 0, HALO, cols1)
     store_kv(kv[HALO * cols1 :], k1, v1, HALO + rows1, HALO, cols1)
 
-    def middle(t, carry):
-        c0 = pl.multiple_of(t * TILE, TILE)
+    for c0 in range(0, cols1, TILE):
         for l0 in range(0, feat1, LANES):
             attend(q1, k1, v1, a1, bias, 0, c0, l0, rows1, me * rows1, n * rows1, cols1)
-        return carry
-
-    lax.fori_loop(0, cols1 // TILE, middle, 0)
     loads[4].wait()
     loads[5].wait()
     y1 = gated(
@@ -401,7 +398,7 @@
         else:
             _, total, summed = lax.fori_loop(0, n // piece, keys_step, start)
         per = block // count2
-        o = (summed / total).reshape(per, count2, 2 * DH)
+        o = (summed * (1.0 / total)).reshape(per, count2, 2 * DH)
         o_out[b * per : (b + 1) * per] = jnp.concatenate(
             [o[:, :pair, DH:], o[:, pair:, DH:]], axis=2
         ).astype(BF16)

time: 38.1 us -> 37.8 us (level)
  no operation moved by 1% of the time
where the time goes in v4:
time: 37.8 us; the launch traced here: 37.6 us
  Pallas kernels  36 us (95%)
  local copies, waits for them, and re-layouts  1.57 us (4%)
    pallas_call x1, Pallas kernels, on_device(): pl.pallas_call(functools.partial(kernel, n), out_shape=jax.ShapeDtypeStru...  36 us
    unnamed x1, local copies, waits for them, and re-layouts  1.57 us

profile of v4, /device:TPU:0, one launch (start us, length us, event | category | flops | bytes accessed | tf_op | source)
XLA Modules:
  0.0 37.6 jit_solution(17526660178858964109)
XLA Ops:
  0.0 36.0 %shard_map.118 = bf16[2,32,1024]{2,1,0:T(8,128)(2,1)} custom-call(bf16[8,128,256]{2,1,0:T(8,128)(2,1)} %tok.1, f32[3,256]{1,0:T(4,128)} %mod0.1, bf16[256,768]{1,0:T(8,128)(2,1)} %w_qkv0.1, bf16[256,256]{1,0:T(8,128)(2,1)} %w_out0.1, bf16[1024,512]{1,0:T(8,128)(2,1)} %w_merge0.1, f32[3,512]{1,0:T(4,128)} %mod1.1, bf16[512,1536]{1,0:T(8,128)(2,1)} %w_qkv1.1, ...), custom_call_target="tpu_custom_call" | custom-call | tf_op jit(solution)/shard_map/pallas_call | solution.py:452
  36.0 1.6 %copy.14 = bf16[2,32,1024]{2,1,0:T(8,128)(2,1)} copy(bf16[2,32,1024]{2,1,0:T(8,128)(2,1)} %shard_map.118) | data formatting | bytes 262144
